TPU v7x, 256 devices: a whole 4x4x8 slice. The times are simulated.
256 devices in a mesh: user: 32 (over z, x), item: 4 (over y), rep: 2 (over core).
Axes of the slice: x: 4, y: 4, z: 8, core: 2. Of those that a mesh axis runs over, the one named last changes fastest.
Arguments:
- item_factors: bfloat16 [131072, 256], P(('user', 'item'))
- user_factors: bfloat16 [4096, 256], P(('user', 'item', 'rep')), may hold values from -6 to 6
- strengths: bfloat16 [4096, 1024], P(('user', 'item', 'rep')), may hold values from 0.5 to 40
- requests: int32 [256, 128], P(('user', 'item', 'rep')), may hold values from -1 to 7, as said below
- user_slots: int32 [4096, 8], P(('user', 'item', 'rep')), may hold values from 0 to 127, as said below
Outputs:
- user_new: float32 [4096, 256], P(('user', 'item', 'rep'))
- item_partial: float32 [131072, 256], P(('user', 'item'))
Inputs may be any that keep to these rules, and one draw needn't show every extreme that they name: `requests`: entry [d, o] names the one tile of owner o that device d reads, or is -1; every row has at least 8 entries that are not -1. `user_slots`: each row holds 8 different owners o, each with requests[u // 16, o] >= 0.
All inputs are finite; a program needn't handle non-finite values.
Results may differ from a plain program's by a relative error of at most 0.0051.
Values may be sent and summed in bfloat16 or wider, within the bound.
No kernel may reach another device: no remote copies, remote signals or barrier semaphores. Data moves between devices by JAX's collectives and lax.ppermute only.
A program may use at most 64 MiB of HBM per device.

v0:
```python
import math
import jax
import jax.numpy as jnp
from jax import lax
from jax.sharding import PartitionSpec as P

TILE = 128
SLOTS_USER = 8
ITERS = 2
penalty = 1.0


def absorb(tiles, gram_matrix, start_rows, strengths, user_slots):
    users = start_rows.shape[0]
    owners = tiles.shape[0]
    factor_dim = tiles.shape[2]
    group = math.gcd(users, 16)
    count = users // group

    def one_group(inputs):
        begin_rows, weight_rows, slot_rows = inputs
        block = tiles[slot_rows].reshape(group, SLOTS_USER * TILE, factor_dim)
        weights = weight_rows.astype(jnp.float32)
        confidence = (1.0 + weights).astype(jnp.bfloat16)
        rhs = jnp.einsum("uj,ujr->ur", confidence, block, preferred_element_type=jnp.float32)

        def against(vectors):
            return jnp.einsum("ur,ujr->uj", vectors, block, preferred_element_type=jnp.float32)

        def operate(vectors):
            scaled = (weights * against(vectors.astype(jnp.bfloat16))).astype(jnp.bfloat16)
            gram_part = jnp.dot(vectors, gram_matrix, precision=lax.Precision.HIGHEST)
            back = jnp.einsum("uj,ujr->ur", scaled, block, preferred_element_type=jnp.float32)
            return gram_part + back + penalty * vectors

        solution = begin_rows.astype(jnp.float32)
        residual = rhs - operate(solution)
        direction = residual
        norm_now = jnp.sum(residual * residual, axis=1, keepdims=True)
        for sweep in range(ITERS):
            image = operate(direction)
            step_size = norm_now / jnp.sum(direction * image, axis=1, keepdims=True)
            solution = solution + step_size * direction
            residual = residual - step_size * image
            norm_next = jnp.sum(residual * residual, axis=1, keepdims=True)
            direction = residual + norm_next / norm_now * direction
            norm_now = norm_next
        solved_rounded = solution.astype(jnp.bfloat16)
        fitted = against(solved_rounded)
        coeffs = (confidence.astype(jnp.float32) - weights * fitted).astype(jnp.bfloat16)
        return (solution, coeffs, solved_rounded)

    solution, coeffs, solved_rounded = lax.map(
        one_group,
        (
            start_rows.reshape(count, group, factor_dim),
            strengths.reshape(count, group, SLOTS_USER * TILE),
            user_slots.reshape(count, group, SLOTS_USER),
        ),
    )
    solution = solution.reshape(users, factor_dim)
    solved_rounded = solved_rounded.reshape(users, factor_dim)
    coeffs = coeffs.reshape(users, SLOTS_USER, TILE)
    onehot = (user_slots[:, :, None] == jnp.arange(owners, dtype=jnp.int32)[None, None, :]).astype(
        jnp.bfloat16
    )
    spread_coeffs = jnp.einsum("uko,ukj->uoj", onehot, coeffs, preferred_element_type=jnp.float32)
    spread_coeffs = spread_coeffs.astype(jnp.bfloat16).reshape(users, owners * TILE)
    return (solution, spread_coeffs, solved_rounded)


def shards(item_factors, user_factors, strengths, requests, user_slots):
    owners = lax.axis_size(("user", "item"))
    tiles_here = item_factors.shape[0] // TILE
    factor_dim = item_factors.shape[1]
    own_tiles = item_factors.reshape(tiles_here, TILE, factor_dim)
    local_gram = jnp.dot(item_factors.T, item_factors, preferred_element_type=jnp.float32)
    gram_matrix = lax.psum(local_gram, ("user", "item"))
    asked_tiles = lax.all_to_all(
        requests.reshape(owners), ("user", "item"), split_axis=0, concat_axis=0, tiled=True
    )
    tile_range = jnp.arange(tiles_here, dtype=jnp.int32)
    pick_float = (asked_tiles[:, None] == tile_range[None, :]).astype(jnp.float32)
    reply_tiles = jnp.einsum(
        "st,tjr->sjr",
        pick_float.astype(jnp.bfloat16),
        own_tiles,
        preferred_element_type=jnp.float32,
    ).astype(jnp.bfloat16)
    fetched = lax.all_to_all(reply_tiles, ("user", "item"), split_axis=0, concat_axis=0, tiled=True)
    solution, coeffs, solved_rounded = absorb(
        fetched, gram_matrix, user_factors, strengths, user_slots
    )
    partial_value = lax.dot_general(
        coeffs, solved_rounded, (((0,), (0,)), ((), ())), preferred_element_type=jnp.float32
    )
    arrived = lax.all_to_all(
        partial_value.reshape(owners, TILE, factor_dim),
        ("user", "item"),
        split_axis=0,
        concat_axis=0,
        tiled=True,
    )
    owned_sums = jnp.einsum("st,sjr->tjr", pick_float, arrived, precision=lax.Precision.HIGHEST)
    item_sums = lax.psum(owned_sums, "rep")
    return (solution, item_sums.reshape(tiles_here * TILE, factor_dim))


def solution(mesh):
    return jax.shard_map(
        shards,
        mesh=mesh,
        in_specs=(
            P(("user", "item"), None),
            P(("user", "item", "rep"), None),
            P(("user", "item", "rep"), None),
            P(("user", "item", "rep"), None),
            P(("user", "item", "rep"), None),
        ),
        out_specs=(P(("user", "item", "rep"), None), P(("user", "item"), None)),
        check_vma=False,
    )
```

profile of v0, /device:TPU:1, one launch (start us, length us, event | category | flops | bytes accessed | tf_op | source)
XLA Modules:
  0.0 765.9 jit_solution(2870779633857930631)
XLA Ops:
  8.0 26.9 %all_to_all.19 = s32[128,1,1]{2,1,0:T(1,128)S(1)} all-to-all(s32[128,1,1]{2,1,0:T(1,128)S(1)} %copy.23), channel_id=1, replica_groups=mesh['user'=32,'item'=4,'rep'=2] {'user','item'}, dimensions={0} | all-to-all | bytes 1024 | tf_op jit(solution)/shard_map/all_to_all | solution.py:79
  34.9 2.3 reduce
  37.2 5.6 convolution_convert_fusion
  42.8 11.4 %copy.25 = bf16[128,128,256]{2,1,0:T(8,128)(2,1)} copy(bf16[128,128,256]{2,0,1:T(8,128)(2,1)} %convolution_convert_fusion) | data formatting | bytes 16777216 | tf_op jit(solution)/shard_map/convert_element_type | solution.py:89
  54.2 7.8 %all-to-all-start.1 = ((bf16[128,128,256]{2,1,0:T(8,128)(2,1)}), bf16[128,128,256]{2,1,0:T(8,128)(2,1)}, u32[]{:S(2)}, u32[]{:S(2)}) async-start(bf16[128,128,256]{2,1,0:T(8,128)(2,1)} %copy.25), calls=%async_computation.1 | async-start | bytes 16777216 | tf_op jit(solution)/shard_map/all_to_all | solution.py:90
  62.0 1.0 fusion.49
  63.4 182.3 %all-to-all-done.1 = bf16[128,128,256]{2,1,0:T(8,128)(2,1)} async-done(((bf16[128,128,256]{2,1,0:T(8,128)(2,1)}), bf16[128,128,256]{2,1,0:T(8,128)(2,1)}, u32[]{:S(2)}, u32[]{:S(2)}) %all-to-all-start.1) | async-done | bytes 8388640 | tf_op jit(solution)/shard_map/all_to_all | solution.py:90
  245.7 10.0 %gather_fusion = bf16[128,128,256]{2,1,0:T(8,128)(2,1)} fusion(bf16[128,128,256]{2,1,0:T(8,128)(2,1)} %all-to-all-done.1, s32[1024]{0:T(1024)S(1)} %pad_clamp_fusion), kind=kCustom, calls=%fused_computation | custom fusion | bytes 16777728 | tf_op jit(solution)/shard_map/while/body/eval_jaxpr/gather | solution.py:22
  255.7 5.8 fusion.40
  261.6 1.2 fusion.25
  262.8 1.2 fusion.23
  264.0 44.8 %all-reduce.3.cloned.1.call-done = f32[256,256]{1,0:T(8,128)} async-done(((f32[256,256]{1,0:T(8,128)}), f32[256,256]{1,0:T(8,128)}) %all-reduce.3.cloned.1.call-update) | async-done | bytes 262160 | tf_op jit(solution)/shard_map/psum | solution.py:78
  308.7 1.2 fusion.7
  309.9 5.6 fusion.38
  315.6 4.7 fusion.21
  321.5 2.3 fusion.36
  323.8 1.2 fusion.19
  326.1 2.3 fusion.34
  328.9 8.1 %fusion.9 = f32[128,128,256]{2,1,0:T(8,128)} fusion(bf16[16,256,1]{1,0,2:T(8,128)(2,1)S(1)} %get-tuple-element.22, bf16[2,8,128,128]{3,2,1,0:T(8,128)(2,1)S(1)} %bitcast.102), kind=kOutput, calls=%fused_computation.16 | convolution fusion | flops 134217728 | bytes 17309696 | tf_op jit(solution)/shard_map/dot_general | solution.py:94
  337.1 367.3 %all_to_all.20 = f32[128,128,256]{2,1,0:T(8,128)S(1)} all-to-all(f32[128,128,256]{2,1,0:T(8,128)} %fusion.9), channel_id=1, replica_groups=mesh['user'=32,'item'=4,'rep'=2] {'user','item'}, dimensions={0} | all-to-all | bytes 33554432 | tf_op jit(solution)/shard_map/all_to_all | solution.py:97
  704.3 15.2 %fusion = f32[8,128,256]{2,0,1:T(8,128)S(1)} fusion(f32[128,128,256]{2,1,0:T(8,128)S(1)} %all_to_all.20, s32[128]{0:T(128)S(1)} %reduce), kind=kOutput, calls=%fused_computation.1 | convolution fusion | flops 402654208 | bytes 17826304 | tf_op jit(solution)/shard_map/st,sjr->tjr/dot_general | solution.py:104
  719.5 1.3 copy.31
  720.8 35.6 %all-reduce.5.cloned.1.call-done = f32[1024,256]{1,0:T(8,128)} async-done(((f32[1024,256]{1,0:T(8,128)}), f32[1024,256]{1,0:T(8,128)}) %all-reduce.5.cloned.1.call-update) | async-done | bytes 1048592 | tf_op jit(solution)/shard_map/psum | solution.py:105
  756.4 2.3 copy.99
  (44 shorter events, 4.2 us)
Async XLA Ops:
  7.2 30.1 %copy-start = (bf16[1024,256]{1,0:T(8,128)(2,1)S(1)}, bf16[1024,256]{1,0:T(8,128)(2,1)}, u32[]{:S(2)}) copy-start(bf16[1024,256]{1,0:T(8,128)(2,1)} %param.5) | copy-start | bytes 1572868
  54.2 9.0 %copy-start.6 = (s32[16,8]{0,1:T(8,128)S(1)}, s32[16,8]{0,1:T(8,128)}, u32[]{:S(2)}) copy-start(s32[16,8]{0,1:T(8,128)} %param.9) | copy-start | bytes 1540
  54.2 191.6 %all-to-all-start.1 = ((bf16[128,128,256]{2,1,0:T(8,128)(2,1)}), bf16[128,128,256]{2,1,0:T(8,128)(2,1)}, u32[]{:S(2)}, u32[]{:S(2)}) async-start(bf16[128,128,256]{2,1,0:T(8,128)(2,1)} %copy.25), calls=%async_computation.1 | async-start | bytes 16777216 | tf_op jit(solution)/shard_map/all_to_all | solution.py:90
  62.0 246.7 %all-reduce.3.cloned.1.call-start = ((), (), s32[]{:S(2)}) async-start(), calls=%async_computation.3 | async-start | bytes 524288 | tf_op jit(solution)/shard_map/psum | solution.py:78
  63.1 693.3 %all-reduce.5.cloned.1.call-start = ((), (), s32[]{:S(2)}) async-start(), calls=%async_computation.4 | async-start | bytes 2097152 | tf_op jit(solution)/shard_map/psum | solution.py:105
  63.4 192.3 %copy-start.5 = (bf16[16,256]{1,0:T(8,128)(2,1)S(1)}, bf16[16,256]{1,0:T(8,128)(2,1)}, u32[]{:S(2)}) copy-start(bf16[16,256]{1,0:T(8,128)(2,1)} %param.6) | copy-start | bytes 24580
  255.7 5.8 copy-start.4
  255.7 5.8 copy-start.2
  315.5 4.8 copy-start.3
  315.5 5.4 slice-start
  315.6 5.9 slice-start.1
  337.1 421.6 %copy-start.1 = (bf16[1024,256]{1,0:T(8,128)(2,1)S(1)}, bf16[1024,256]{1,0:T(8,128)(2,1)}, u32[]{:S(2)}) copy-start(bf16[1024,256]{1,0:T(8,128)(2,1)} %param.5) | copy-start | bytes 1572868
Sparse Core Ops, SparseCore 0:
  68.8 239.8 all-reduce.2
  721.0 35.3 all-reduce.4
where the time goes:
time: 775 us; the launch traced here: 766 us
  blocking collectives  394 us (51%)
  waiting for transfers between devices  263 us (34%)
  matrix products  56.6 us (7%)
  local copies, waits for them, and re-layouts  26.5 us (3%)
  between operations  14.6 us (2%)
  starting transfers between devices  7.87 us (1%)
    all_to_all x1, blocking collectives, shards(): lax.all_to_all(partial_value.reshape(owners, TILE, factor_dim), ('user',...  367 us
    all_to_all x1, waiting for transfers between devices, shards(): lax.all_to_all(reply_tiles, ('user', 'item'), split_axis=0, concat_axis=0...  182 us
    psum x1, waiting for transfers between devices, shards(): gram_matrix = lax.psum(local_gram, ('user', 'item'))  44.8 us
    psum x1, waiting for transfers between devices, shards(): item_sums = lax.psum(owned_sums, 'rep')  35.6 us
    all_to_all x1, blocking collectives, shards(): lax.all_to_all(requests.reshape(owners), ('user', 'item'), split_axis=0,...  26.9 us
    dot_general x4, matrix products, against(): jnp.einsum('ur,ujr->uj', vectors, block, preferred_element_type=jnp.float32)  15.9 us
  transfers between devices with their start and end apart: 3, of which 3 were waited for; matrix products, arithmetic and copies ran while one was open for 3% of the time, Pallas kernels for 0%

commit v1 on v0

--- a/solution.py
+++ b/solution.py
@@ -75,7 +75,7 @@
     factor_dim = item_factors.shape[1]
     own_tiles = item_factors.reshape(tiles_here, TILE, factor_dim)
     local_gram = jnp.dot(item_factors.T, item_factors, preferred_element_type=jnp.float32)
-    gram_matrix = lax.psum(local_gram, ("user", "item"))
+    gram_matrix = lax.psum(lax.psum(local_gram, "user"), "item")
     asked_tiles = lax.all_to_all(
         requests.reshape(owners), ("user", "item"), split_axis=0, concat_axis=0, tiled=True
     )

time: 775 us -> 748 us (0.965)
  waiting for transfers between devices: 263 us -> 229 us
    all_to_all x1, waiting for transfers between devices: 182 us -> 18.9 us  [shards(): lax.all_to_all(reply_tiles, ('user', 'item'), split_axis=0, concat_axis=0...]
    psum x1 -> x2, waiting for transfers between devices: 44.8 us -> 178 us  [shards(): gram_matrix = lax.psum(lax.psum(local_gram, 'user'), 'item')]
  transfers between devices with their start and end apart: 3 -> 4, of which waited for: 3 -> 4; matrix products, arithmetic and copies ran while one was open for 3% -> 3% of each run, Pallas kernels for 0% -> 0%
where the time goes in v1:
time: 748 us; the launch traced here: 739 us
  blocking collectives  401 us (54%)
  waiting for transfers between devices  229 us (31%)
  matrix products  56.6 us (8%)
  local copies, waits for them, and re-layouts  26.5 us (4%)
  between operations  14.3 us (2%)
  starting transfers between devices  7.9 us (1%)
    all_to_all x1, blocking collectives, shards(): lax.all_to_all(partial_value.reshape(owners, TILE, factor_dim), ('user',...  374 us
    psum x2, waiting for transfers between devices, shards(): gram_matrix = lax.psum(lax.psum(local_gram, 'user'), 'item')  178 us
    psum x1, waiting for transfers between devices, shards(): item_sums = lax.psum(owned_sums, 'rep')  32.4 us
    all_to_all x1, blocking collectives, shards(): lax.all_to_all(requests.reshape(owners), ('user', 'item'), split_axis=0,...  26.9 us
    all_to_all x1, waiting for transfers between devices, shards(): lax.all_to_all(reply_tiles, ('user', 'item'), split_axis=0, concat_axis=0...  18.9 us
    dot_general x4, matrix products, against(): jnp.einsum('ur,ujr->uj', vectors, block, preferred_element_type=jnp.float32)  15.9 us
    dot_general x1, matrix products, shards(): jnp.einsum('st,sjr->tjr', pick_float, arrived, precision=lax.Precision.HI...  15.2 us
  transfers between devices with their start and end apart: 4, of which 4 were waited for; matrix products, arithmetic and copies ran while one was open for 3% of the time, Pallas kernels for 0%

profile of v1, /device:TPU:1, one launch (start us, length us, event | category | flops | bytes accessed | tf_op | source)
XLA Modules:
  0.0 739.1 jit_solution(11425159816170331128)
XLA Ops:
  8.0 26.9 %all_to_all.19 = s32[128,1,1]{2,1,0:T(1,128)S(1)} all-to-all(s32[128,1,1]{2,1,0:T(1,128)S(1)} %copy.23), channel_id=1, replica_groups=mesh['user'=32,'item'=4,'rep'=2] {'user','item'}, dimensions={0} | all-to-all | bytes 1024 | tf_op jit(solution)/shard_map/all_to_all | solution.py:79
  34.9 2.3 reduce
  37.2 5.6 convolution_convert_fusion
  42.8 11.4 %copy.25 = bf16[128,128,256]{2,1,0:T(8,128)(2,1)} copy(bf16[128,128,256]{2,0,1:T(8,128)(2,1)} %convolution_convert_fusion) | data formatting | bytes 16777216 | tf_op jit(solution)/shard_map/convert_element_type | solution.py:89
  54.2 7.8 %all-to-all-start.1 = ((bf16[128,128,256]{2,1,0:T(8,128)(2,1)}), bf16[128,128,256]{2,1,0:T(8,128)(2,1)}, u32[]{:S(2)}, u32[]{:S(2)}) async-start(bf16[128,128,256]{2,1,0:T(8,128)(2,1)} %copy.25), calls=%async_computation.1 | async-start | bytes 16777216 | tf_op jit(solution)/shard_map/all_to_all | solution.py:90
  63.4 165.0 %all-reduce.4.cloned.1.call-done = f32[256,256]{1,0:T(8,128)} async-done(((f32[256,256]{1,0:T(8,128)}), f32[256,256]{1,0:T(8,128)}) %all-reduce.4.cloned.1.call-update) | async-done | bytes 262160 | tf_op jit(solution)/shard_map/psum | solution.py:78
  228.5 18.9 %all-to-all-done.1 = bf16[128,128,256]{2,1,0:T(8,128)(2,1)} async-done(((bf16[128,128,256]{2,1,0:T(8,128)(2,1)}), bf16[128,128,256]{2,1,0:T(8,128)(2,1)}, u32[]{:S(2)}, u32[]{:S(2)}) %all-to-all-start.1) | async-done | bytes 8388640 | tf_op jit(solution)/shard_map/all_to_all | solution.py:90
  247.4 10.0 %gather_fusion = bf16[128,128,256]{2,1,0:T(8,128)(2,1)} fusion(bf16[128,128,256]{2,1,0:T(8,128)(2,1)} %all-to-all-done.1, s32[1024]{0:T(1024)S(1)} %pad_clamp_fusion), kind=kCustom, calls=%fused_computation | custom fusion | bytes 16777728 | tf_op jit(solution)/shard_map/while/body/eval_jaxpr/gather | solution.py:22
  257.4 5.8 fusion.40
  263.2 1.2 fusion.25
  264.4 1.2 fusion.23
  265.6 12.9 %all-reduce.6.cloned.1.call-done = f32[256,256]{1,0:T(8,128)} async-done(((f32[256,256]{1,0:T(8,128)}), f32[256,256]{1,0:T(8,128)}) %all-reduce.6.cloned.1.call-update) | async-done | bytes 262160 | tf_op jit(solution)/shard_map/psum | solution.py:78
  278.5 1.2 fusion.7
  279.7 5.6 fusion.38
  285.4 4.7 fusion.21
  291.3 2.3 fusion.36
  293.6 1.2 fusion.19
  295.8 2.3 fusion.34
  298.7 8.1 %fusion.9 = f32[128,128,256]{2,1,0:T(8,128)} fusion(bf16[16,256,1]{1,0,2:T(8,128)(2,1)S(1)} %get-tuple-element.22, bf16[2,8,128,128]{3,2,1,0:T(8,128)(2,1)S(1)} %bitcast.102), kind=kOutput, calls=%fused_computation.16 | convolution fusion | flops 134217728 | bytes 17309696 | tf_op jit(solution)/shard_map/dot_general | solution.py:94
  306.8 374.1 %all_to_all.20 = f32[128,128,256]{2,1,0:T(8,128)S(1)} all-to-all(f32[128,128,256]{2,1,0:T(8,128)} %fusion.9), channel_id=1, replica_groups=mesh['user'=32,'item'=4,'rep'=2] {'user','item'}, dimensions={0} | all-to-all | bytes 33554432 | tf_op jit(solution)/shard_map/all_to_all | solution.py:97
  681.0 15.2 %fusion = f32[8,128,256]{2,0,1:T(8,128)S(1)} fusion(f32[128,128,256]{2,1,0:T(8,128)S(1)} %all_to_all.20, s32[128]{0:T(128)S(1)} %reduce), kind=kOutput, calls=%fused_computation.1 | convolution fusion | flops 402654208 | bytes 17826304 | tf_op jit(solution)/shard_map/st,sjr->tjr/dot_general | solution.py:104
  696.1 1.3 copy.31
  697.5 32.4 %all-reduce.8.cloned.1.call-done = f32[1024,256]{1,0:T(8,128)} async-done(((f32[1024,256]{1,0:T(8,128)}), f32[1024,256]{1,0:T(8,128)}) %all-reduce.8.cloned.1.call-update) | async-done | bytes 1048592 | tf_op jit(solution)/shard_map/psum | solution.py:105
  729.8 2.3 copy.100
  (47 shorter events, 5.3 us)
Async XLA Ops:
  7.2 30.1 %copy-start = (bf16[1024,256]{1,0:T(8,128)(2,1)S(1)}, bf16[1024,256]{1,0:T(8,128)(2,1)}, u32[]{:S(2)}) copy-start(bf16[1024,256]{1,0:T(8,128)(2,1)} %param.5) | copy-start | bytes 1572868
  54.2 9.0 %copy-start.6 = (s32[16,8]{0,1:T(8,128)S(1)}, s32[16,8]{0,1:T(8,128)}, u32[]{:S(2)}) copy-start(s32[16,8]{0,1:T(8,128)} %param.9) | copy-start | bytes 1540
  54.2 193.2 %all-to-all-start.1 = ((bf16[128,128,256]{2,1,0:T(8,128)(2,1)}), bf16[128,128,256]{2,1,0:T(8,128)(2,1)}, u32[]{:S(2)}, u32[]{:S(2)}) async-start(bf16[128,128,256]{2,1,0:T(8,128)(2,1)} %copy.25), calls=%async_computation.1 | async-start | bytes 16777216 | tf_op jit(solution)/shard_map/all_to_all | solution.py:90
  62.0 166.4 %all-reduce.4.cloned.1.call-start = ((), (), s32[]{:S(2)}) async-start(), calls=%async_computation.3 | async-start | bytes 524288 | tf_op jit(solution)/shard_map/psum | solution.py:78
  63.1 215.4 %all-reduce.6.cloned.1.call-start = ((), (), s32[]{:S(2)}) async-start(), calls=%async_computation.4 | async-start | bytes 524288 | tf_op jit(solution)/shard_map/psum | solution.py:78
  228.4 29.0 %copy-start.5 = (bf16[16,256]{1,0:T(8,128)(2,1)S(1)}, bf16[16,256]{1,0:T(8,128)(2,1)}, u32[]{:S(2)}) copy-start(bf16[16,256]{1,0:T(8,128)(2,1)} %param.6) | copy-start | bytes 24580
  228.4 501.4 %all-reduce.8.cloned.1.call-start = ((), (), s32[]{:S(2)}) async-start(), calls=%async_computation.5 | async-start | bytes 2097152 | tf_op jit(solution)/shard_map/psum | solution.py:105
  257.4 5.8 copy-start.4
  257.4 5.8 copy-start.2
  285.3 4.8 copy-start.3
  285.3 5.4 slice-start
  285.4 5.9 slice-start.1
  306.8 425.3 %copy-start.1 = (bf16[1024,256]{1,0:T(8,128)(2,1)S(1)}, bf16[1024,256]{1,0:T(8,128)(2,1)}, u32[]{:S(2)}) copy-start(bf16[1024,256]{1,0:T(8,128)(2,1)} %param.5) | copy-start | bytes 1572868
Sparse Core Ops, SparseCore 0:
  66.8 161.4 all-reduce.3
  230.7 47.7 all-reduce.5
  697.6 32.2 all-reduce.7

commit v2 on v0

--- a/solution.py
+++ b/solution.py
@@ -75,7 +75,7 @@
     factor_dim = item_factors.shape[1]
     own_tiles = item_factors.reshape(tiles_here, TILE, factor_dim)
     local_gram = jnp.dot(item_factors.T, item_factors, preferred_element_type=jnp.float32)
-    gram_matrix = lax.psum(local_gram, ("user", "item"))
+    gram_matrix = jnp.sum(lax.all_gather(local_gram, ("user", "item")), axis=0)
     asked_tiles = lax.all_to_all(
         requests.reshape(owners), ("user", "item"), split_axis=0, concat_axis=0, tiled=True
     )

time: 775 us -> 858 us (1.11)
  waiting for transfers between devices: 263 us -> 326 us
  other arithmetic: 3.46 us -> 15.4 us
    all_to_all x1, waiting for transfers between devices: 182 us -> 246 us  [shards(): lax.all_to_all(reply_tiles, ('user', 'item'), split_axis=0, concat_axis=0...]
    all_gather x0 -> x1, waiting for transfers between devices: none -> 49.5 us  [shards(): gram_matrix = jnp.sum(lax.all_gather(local_gram, ('user', 'item')), axis=0)]
    psum x1 -> x0, waiting for transfers between devices: 44.8 us -> none  [shards(): gram_matrix = lax.psum(local_gram, ('user', 'item'))]
    reduce_sum x0 -> x1, other arithmetic: none -> 12 us  [shards(): gram_matrix = jnp.sum(lax.all_gather(local_gram, ('user', 'item')), axis=0)]
  transfers between devices with their start and end apart: 3 -> 3, of which waited for: 3 -> 3; matrix products, arithmetic and copies ran while one was open for 3% -> 5% of each run, Pallas kernels for 0% -> 0%
where the time goes in v2:
time: 858 us; the launch traced here: 849 us
  blocking collectives  402 us (47%)
  waiting for transfers between devices  326 us (38%)
  matrix products  55.8 us (7%)
  local copies, waits for them, and re-layouts  27.8 us (3%)
  other arithmetic  15.4 us (2%)
  between operations  14.6 us (2%)
    all_to_all x1, blocking collectives, shards(): lax.all_to_all(partial_value.reshape(owners, TILE, factor_dim), ('user',...  375 us
    all_to_all x1, waiting for transfers between devices, shards(): lax.all_to_all(reply_tiles, ('user', 'item'), split_axis=0, concat_axis=0...  246 us
    all_gather x1, waiting for transfers between devices, shards(): gram_matrix = jnp.sum(lax.all_gather(local_gram, ('user', 'item')), axis=0)  49.5 us
    psum x1, waiting for transfers between devices, shards(): item_sums = lax.psum(owned_sums, 'rep')  29.7 us
    all_to_all x1, blocking collectives, shards(): lax.all_to_all(requests.reshape(owners), ('user', 'item'), split_axis=0,...  26.9 us
  transfers between devices with their start and end apart: 3, of which 3 were waited for; matrix products, arithmetic and copies ran while one was open for 5% of the time, Pallas kernels for 0%

profile of v2, /device:TPU:1, one launch (start us, length us, event | category | flops | bytes accessed | tf_op | source)
XLA Modules:
  0.0 848.9 jit_solution(16510684455101726185)
XLA Ops:
  8.2 1.0 fusion.49
  10.0 26.9 %all_to_all.19 = s32[128,1,1]{2,1,0:T(1,128)S(1)} all-to-all(s32[128,1,1]{2,1,0:T(1,128)S(1)} %copy.23), channel_id=1, replica_groups=mesh['user'=32,'item'=4,'rep'=2] {'user','item'}, dimensions={0} | all-to-all | bytes 1024 | tf_op jit(solution)/shard_map/all_to_all | solution.py:79
  36.9 2.3 reduce
  39.3 5.6 convolution_convert_fusion
  44.9 11.4 %copy.25 = bf16[128,128,256]{2,1,0:T(8,128)(2,1)} copy(bf16[128,128,256]{2,0,1:T(8,128)(2,1)} %convolution_convert_fusion) | data formatting | bytes 16777216 | tf_op jit(solution)/shard_map/convert_element_type | solution.py:89
  56.2 7.8 all-to-all-start.1
  64.4 246.5 %all-to-all-done.1 = bf16[128,128,256]{2,1,0:T(8,128)(2,1)} async-done(((bf16[128,128,256]{2,1,0:T(8,128)(2,1)}), bf16[128,128,256]{2,1,0:T(8,128)(2,1)}, u32[]{:S(2)}, u32[]{:S(2)}) %all-to-all-start.1) | async-done | bytes 8388640 | tf_op jit(solution)/shard_map/all_to_all | solution.py:90
  310.9 10.4 %gather_fusion = bf16[128,128,256]{2,1,0:T(8,128)(2,1)} fusion(bf16[128,128,256]{2,1,0:T(8,128)(2,1)} %all-to-all-done.1, s32[1024]{0:T(1024)S(1)} %pad_clamp_fusion), kind=kCustom, calls=%fused_computation | custom fusion | bytes 16777728 | tf_op jit(solution)/shard_map/while/body/eval_jaxpr/gather | solution.py:22
  321.3 6.0 fusion.40
  327.3 1.2 fusion.23
  328.4 1.2 fusion.25
  329.6 49.5 %all-gather.3.cloned.1.call-done = f32[32768,256]{1,0:T(8,128)} async-done(((f32[256,256]{1,0:T(8,128)}), f32[32768,256]{1,0:T(8,128)}) %all-gather.3.cloned.1.call-update) | async-done | bytes 33554448 | tf_op jit(solution)/shard_map/all_gather | solution.py:78
  379.2 12.0 %reduce_sum.49 = f32[256,256]{1,0:T(8,128)S(1)} reduce(f32[128,256,256]{2,1,0:T(8,128)} %bitcast.102, f32[]{:T(128)} %constant.18.clone.1), dimensions={0}, to_apply=%region_0.0 | reduce | flops 8323072 | bytes 33816580 | tf_op jit(solution)/shard_map/reduce_sum | solution.py:78
  391.4 5.6 fusion.38
  397.1 4.7 fusion.21
  402.9 2.3 fusion.36
  405.2 1.2 fusion.19
  407.4 2.3 fusion.34
  410.3 8.1 fusion.9
  418.4 374.7 %all_to_all.20 = f32[128,128,256]{2,1,0:T(8,128)S(1)} all-to-all(f32[128,128,256]{2,1,0:T(8,128)} %fusion.9), channel_id=1, replica_groups=mesh['user'=32,'item'=4,'rep'=2] {'user','item'}, dimensions={0} | all-to-all | bytes 33554432 | tf_op jit(solution)/shard_map/all_to_all | solution.py:97
  793.1 15.2 %fusion = f32[8,128,256]{2,0,1:T(8,128)S(1)} fusion(f32[128,128,256]{2,1,0:T(8,128)S(1)} %all_to_all.20, s32[128]{0:T(128)S(1)} %reduce), kind=kOutput, calls=%fused_computation.1 | convolution fusion | flops 402654208 | bytes 17826304 | tf_op jit(solution)/shard_map/st,sjr->tjr/dot_general | solution.py:104
  808.3 1.3 copy.31
  809.6 29.7 %all-reduce.2.cloned.1.call-done = f32[1024,256]{1,0:T(8,128)} async-done(((f32[1024,256]{1,0:T(8,128)}), f32[1024,256]{1,0:T(8,128)}) %all-reduce.2.cloned.1.call-update) | async-done | bytes 1048592 | tf_op jit(solution)/shard_map/psum | solution.py:105
  839.3 2.3 copy.98
  (43 shorter events, 5.2 us)
Async XLA Ops:
  7.2 1.1 copy-start
  7.2 372.0 %all-gather.3.cloned.1.call-start = ((), (), s32[]{:S(2)}) async-start(), calls=%async_computation.4 | async-start | bytes 33816576 | tf_op jit(solution)/shard_map/all_gather | solution.py:78
  56.2 7.9 copy-start.5
  56.2 254.6 %all-to-all-start.1 = ((bf16[128,128,256]{2,1,0:T(8,128)(2,1)}), bf16[128,128,256]{2,1,0:T(8,128)(2,1)}, u32[]{:S(2)}, u32[]{:S(2)}) async-start(bf16[128,128,256]{2,1,0:T(8,128)(2,1)} %copy.25), calls=%async_computation.1 | async-start | bytes 16777216 | tf_op jit(solution)/shard_map/all_to_all | solution.py:90
  64.0 775.3 %all-reduce.2.cloned.1.call-start = ((), (), s32[]{:S(2)}) async-start(), calls=%async_computation.3 | async-start | bytes 2097152 | tf_op jit(solution)/shard_map/psum | solution.py:105
  64.4 256.9 %copy-start.4 = (bf16[16,256]{1,0:T(8,128)(2,1)S(1)}, bf16[16,256]{1,0:T(8,128)(2,1)}, u32[]{:S(2)}) copy-start(bf16[16,256]{1,0:T(8,128)(2,1)} %param.6) | copy-start | bytes 24580
  321.2 6.0 copy-start.3
  321.2 6.0 copy-start.2
  397.0 5.4 slice-start
  397.0 5.8 slice-start.1
  418.4 423.2 %copy-start.1 = (bf16[1024,256]{1,0:T(8,128)(2,1)S(1)}, bf16[1024,256]{1,0:T(8,128)(2,1)}, u32[]{:S(2)}) copy-start(bf16[1024,256]{1,0:T(8,128)(2,1)} %param.5) | copy-start | bytes 1572868
Sparse Core Ops, SparseCore 0:
  12.1 367.0 all-gather.2
  809.8 29.5 all-reduce.1
